TPU v7x, 32 devices: a whole 2x2x4 slice. The times are simulated.
32 devices in a mesh: dp: 1, dap: 32 (over z, y, x, core).
Axes of the slice: x: 2, y: 2, z: 4, core: 2. Of those that a mesh axis runs over, the one named last changes fastest.
Arguments:
- alignment: bfloat16 [128, 256, 256], P(('dp', 'dap')), may hold values from -6 to 6
- pair_rep: bfloat16 [256, 256, 128], P(('dp', 'dap')), may hold values from -6 to 6
- align_mask: int32 [128, 256], P(('dp', 'dap')), may hold values 0 or 1
- residue_mask: int32 [256], P('dp'), may hold values 0 or 1
- row_gain: float32 [256], replicated, may hold values from 0.1 to 1.9
- pair_gain: float32 [128], replicated, may hold values from 0.1 to 1.9
- row_bias: bfloat16 [128, 8], replicated, may hold values from -0.5 to 0.5
- row_scoring: bfloat16 [256, 512], replicated, may hold values from -4 to 4
- row_values: bfloat16 [256, 512], replicated, may hold values from -0.375 to 0.375
- row_output: bfloat16 [256, 256], replicated, may hold values from -0.375 to 0.375
- column_gain: float32 [256], replicated, may hold values from 0.1 to 1.9
- column_scoring: bfloat16 [256, 512], replicated, may hold values from -4 to 4
- column_values: bfloat16 [256, 512], replicated, may hold values from -0.375 to 0.375
- column_output: bfloat16 [256, 256], replicated, may hold values from -0.375 to 0.375
- outer_gain: float32 [256], replicated, may hold values from 0.1 to 1.9
- outer_inputs: bfloat16 [256, 64], replicated, may hold values from -0.375 to 0.375
- outer_output: bfloat16 [1024, 128], replicated, may hold values from -1 to 1
Outputs:
- new_alignment: bfloat16 [128, 256, 256], P(('dp', 'dap'))
- new_pair: bfloat16 [256, 256, 128], P(('dp', 'dap'))
All inputs are finite; a program needn't handle non-finite values. No bound on the sum of `align_mask` on one device may be relied on, other than what follows from the above.
Results may differ from a plain program's by a relative error of at most 0.012.
The roundings to bfloat16 on the way count: a program that leaves them out, or rounds other values in their place, can miss the bound.
Values may be sent and summed in bfloat16 or wider, within the bound.
A program may use at most 64 MiB of HBM per device.

v0:
```python
import math

import jax
import jax.numpy as jnp
from jax import lax
from jax.sharding import PartitionSpec as P

HEADS = 8
HEAD = 32
C_OPM = 32


def layer_norm(values_in, gain):
    wide = values_in.astype(jnp.float32)
    average = jnp.mean(wide, axis=-1, keepdims=True)
    centred = wide - average
    spread = jnp.mean(centred * centred, axis=-1, keepdims=True)
    return (centred * lax.rsqrt(spread + 1e-05) * gain).astype(jnp.bfloat16)


def linear(inputs, weight):
    return jnp.einsum("...c,cd->...d", inputs, weight, preferred_element_type=jnp.float32)


def split_heads(tensor):
    return tensor.reshape(tensor.shape[:2] + (HEADS, HEAD))


def row_attend(queries, keys_all, values_all, gates, keep_mask, bias_term):
    scores = jnp.einsum(
        "sihd,sjhd->shij",
        split_heads(queries),
        split_heads(keys_all),
        preferred_element_type=jnp.float32,
    )
    scores = scores / math.sqrt(HEAD) + bias_term[None]
    scores = jnp.where(keep_mask[:, None, None, :] > 0, scores, -1000000000.0)
    weights = jax.nn.softmax(scores, axis=-1).astype(jnp.bfloat16)
    mixed = jnp.einsum(
        "shij,sjhd->sihd", weights, split_heads(values_all), preferred_element_type=jnp.float32
    )
    mixed = mixed.reshape(queries.shape)
    return (mixed * jax.nn.sigmoid(gates.astype(jnp.float32))).astype(jnp.bfloat16)


def column_attend(queries, keys_all, values_all, gates, keep_mask):
    scores = jnp.einsum(
        "srhd,trhd->rhst",
        split_heads(queries),
        split_heads(keys_all),
        preferred_element_type=jnp.float32,
    )
    scores = scores / math.sqrt(HEAD)
    keep_turned = jnp.swapaxes(keep_mask, 0, 1)
    scores = jnp.where(keep_turned[:, None, None, :] > 0, scores, -1000000000.0)
    weights = jax.nn.softmax(scores, axis=-1).astype(jnp.bfloat16)
    mixed = jnp.einsum(
        "rhst,trhd->srhd", weights, split_heads(values_all), preferred_element_type=jnp.float32
    )
    mixed = mixed.reshape(queries.shape)
    return (mixed * jax.nn.sigmoid(gates.astype(jnp.float32))).astype(jnp.bfloat16)


def body(
    alignment,
    pair_rep,
    align_mask,
    residue_mask,
    row_gain,
    pair_gain,
    row_bias,
    row_scoring,
    row_values,
    row_output,
    column_gain,
    column_scoring,
    column_values,
    column_output,
    outer_gain,
    outer_inputs,
    outer_output,
):
    channels = alignment.shape[2]
    rows_here = pair_rep.shape[0]
    mask_float = align_mask.astype(jnp.float32)
    mask_narrow = align_mask.astype(jnp.bfloat16)
    residue_float = residue_mask.astype(jnp.float32)
    pair_bias = jnp.einsum(
        "ijz,zh->hij", layer_norm(pair_rep, pair_gain), row_bias, preferred_element_type=jnp.float32
    ).astype(jnp.bfloat16)
    normed = layer_norm(alignment, row_gain)
    joint = linear(normed, row_scoring).astype(jnp.bfloat16)
    gated = linear(normed, row_values).astype(jnp.bfloat16)
    queries, keys_all = (joint[..., :channels], joint[..., channels:])
    values_all, gates = (gated[..., :channels], gated[..., channels:])
    keep_rows = mask_float * residue_float[None, :]
    mixed = row_attend(
        queries,
        keys_all,
        values_all,
        gates,
        keep_rows,
        lax.all_gather(pair_bias, "dap", axis=1, tiled=True).astype(jnp.float32),
    )
    row_update = linear(mixed, row_output)
    first_update = (alignment.astype(jnp.float32) + row_update).astype(jnp.bfloat16)
    columns, column_keep = (
        lax.all_to_all(first_update, "dap", split_axis=1, concat_axis=0, tiled=True),
        lax.all_to_all(mask_narrow, "dap", split_axis=1, concat_axis=0, tiled=True),
    )
    keep_columns = column_keep.astype(jnp.float32)
    column_normed = layer_norm(columns, column_gain)
    column_joint = linear(column_normed, column_scoring).astype(jnp.bfloat16)
    column_gated = linear(column_normed, column_values).astype(jnp.bfloat16)
    column_mixed = column_attend(
        column_joint[..., :channels],
        column_joint[..., channels:],
        column_gated[..., :channels],
        column_gated[..., channels:],
        keep_columns,
    )
    second_update = (columns.astype(jnp.float32) + linear(column_mixed, column_output)).astype(
        jnp.bfloat16
    )
    new_alignment = lax.all_to_all(second_update, "dap", split_axis=0, concat_axis=1, tiled=True)
    outer_normed = layer_norm(new_alignment, outer_gain)
    sides = (linear(outer_normed, outer_inputs) * mask_float[..., None]).astype(jnp.bfloat16)
    left_side = lax.all_to_all(sides[..., :C_OPM], "dap", split_axis=1, concat_axis=0, tiled=True)
    right_side, right_keep = (
        lax.all_gather(sides[..., C_OPM:], "dap", axis=0, tiled=True),
        lax.all_gather(mask_narrow, "dap", axis=0, tiled=True),
    )
    pair_count = jnp.dot(
        jnp.swapaxes(column_keep, 0, 1), right_keep, preferred_element_type=jnp.float32
    )
    total_res = right_side.shape[1]
    span = math.gcd(total_res, 128)
    block_count = total_res // span
    right_blocks = jnp.moveaxis(
        right_side.reshape(right_side.shape[0], block_count, span, C_OPM), 1, 0
    )

    def outer_block(right_piece):
        products = jnp.einsum(
            "sic,sje->ijce", left_side, right_piece, preferred_element_type=jnp.float32
        ).astype(jnp.bfloat16)
        flat = products.reshape(rows_here, span, C_OPM * C_OPM)
        return linear(flat, outer_output)

    outer_rows = lax.map(outer_block, right_blocks)
    outer_rows = jnp.moveaxis(outer_rows, 0, 1).reshape(rows_here, total_res, outer_output.shape[1])
    offset = lax.axis_index("dap") * rows_here
    row_factor = lax.dynamic_slice_in_dim(residue_float, offset, rows_here)
    scaled = (
        outer_rows
        / (0.001 + pair_count)[..., None]
        * row_factor[:, None, None]
        * residue_float[None, :, None]
    )
    new_pair = (pair_rep.astype(jnp.float32) + scaled).astype(jnp.bfloat16)
    return (new_alignment, new_pair)


def solution(mesh):
    in_specs = (
        P(("dp", "dap"), None, None),
        P(("dp", "dap"), None, None),
        P(("dp", "dap"), None),
        P("dp"),
        P(),
        P(),
        P(),
        P(),
        P(),
        P(),
        P(),
        P(),
        P(),
        P(),
        P(),
        P(),
        P(),
    )
    out_specs = (P(("dp", "dap"), None, None), P(("dp", "dap"), None, None))
    return jax.shard_map(body, mesh=mesh, in_specs=in_specs, out_specs=out_specs, check_vma=False)
```

profile of v0, /device:TPU:0, one launch (start us, length us, event | category | flops | bytes accessed | tf_op | source)
XLA Modules:
  0.0 223.3 jit_solution(6364969437507721524)
XLA Ops:
  7.2 1.3 convert_reduce_fusion
  8.5 1.7 fusion.27
  10.3 2.5 %fusion.26 = bf16[8,8,256]{2,0,1:T(8,128)(2,1)} fusion(bf16[8,256,128]{2,1,0:T(8,128)(2,1)} %param.20, f32[128]{0:T(128)} %param.24, f32[8,256]{1,0:T(8,128)S(1)} %add_rsqrt_fusion.2, f32[8,256]{1,0:T(8,128)S(1)} %broadcast_multiply_fusion.2, bf16[128,8]{0,1:T(8,128)(2,1)} %param.25), kind=kOutput, calls=%fused_computation.50 | convolution fusion | flops 5521408 | bytes 576000 | tf_op jit(solution)/shard_map/ijz,zh->hij/dot_general | solution.py:88
  12.7 0.8 fusion.72
  13.6 0.6 copy.118
  14.2 7.3 %all-to-all-start.1 = ((bf16[4,32,8]{2,0,1:T(4,128)(2,1)}), bf16[4,32,8]{2,0,1:T(4,128)(2,1)S(1)}, u32[]{:S(2)}, u32[]{:S(2)}) async-start(bf16[4,32,8]{2,0,1:T(4,128)(2,1)} %copy.118), calls=%async_computation.1 | async-start | bytes 65536 | tf_op jit(solution)/shard_map/all_to_all | solution.py:109
  21.5 1.3 convert_reduce_fusion.1
  22.8 1.4 fusion.30
  24.3 1.5 convolution_convert_fusion.2
  25.9 0.2 copy.102
  26.1 1.0 copy.103
  27.1 0.5 convolution_convert_fusion.3
  27.7 1.1 copy.101
  28.8 40.5 %all-gather.4.cloned.1.call-done = bf16[8,256,256]{2,0,1:T(8,128)(2,1)} async-done(((bf16[8,8,256]{2,0,1:T(8,128)(2,1)}), bf16[8,256,256]{2,0,1:T(8,128)(2,1)}) %all-gather.4.cloned.1.call-update) | async-done | bytes 1048592 | tf_op jit(solution)/shard_map/all_gather | solution.py:103
  69.3 1.9 copy.104
  71.1 7.6 %fusion.73 = (f32[4,8,256]{2,1,0:T(8,128)S(1)}, f32[4,8,256,256]{2,3,1,0:T(8,128)}) fusion(f32[8,256,256]{1,2,0:T(8,128)S(1)} %copy.104, pred[4,256]{1,0:T(4,128)(4,1)S(1)} %multiply_compare_fusion, bf16[4,256,8,32]{1,3,2,0:T(8,128)(2,1)S(1)} %bitcast.152, bf16[4,256,8,32]{1,3,2,0:T(8,128)(2,1)} %bitcast.153), kind=kOutput, calls=%fused_computation.113 | convolution fusion | flops 144703744 | bytes 11568128 | tf_op jit(solution)/shard_map/sub | solution.py:38
  78.8 4.4 %fusion.13 = f32[4,8,32,256]{3,2,1,0:T(8,128)S(1)} fusion(bf16[4,256,8,32]{1,3,2,0:T(8,128)(2,1)} %bitcast.154, f32[4,8,256,256]{2,3,1,0:T(8,128)} %get-tuple-element.64, f32[4,8,256]{2,1,0:T(8,128)S(1)} %get-tuple-element.63), kind=kOutput, calls=%fused_computation.21 | convolution fusion | flops 138412032 | bytes 9994240 | tf_op jit(solution)/shard_map/shij,sjhd->sihd/dot_general | solution.py:39
  83.2 0.3 copy.106
  83.6 1.5 fusion.19
  85.0 1.2 copy.107
  86.2 3.6 %all-to-all-start = ((bf16[4,256,256]{2,0,1:T(4,128)(2,1)}), bf16[4,256,256]{2,0,1:T(4,128)(2,1)S(1)}, u32[]{:S(2)}, u32[]{:S(2)}) async-start(bf16[4,256,256]{2,0,1:T(4,128)(2,1)} %copy.107), calls=%async_computation | async-start | bytes 1048576 | tf_op jit(solution)/shard_map/all_to_all | solution.py:108
  89.8 0.2 all-gather.6.cloned.1.call-start
  90.1 15.2 %all-to-all-done = bf16[4,256,256]{2,0,1:T(4,128)(2,1)S(1)} async-done(((bf16[4,256,256]{2,0,1:T(4,128)(2,1)}), bf16[4,256,256]{2,0,1:T(4,128)(2,1)S(1)}, u32[]{:S(2)}, u32[]{:S(2)}) %all-to-all-start) | async-done | bytes 524320 | tf_op jit(solution)/shard_map/all_to_all | solution.py:108
  105.5 0.2 fusion.68
  105.8 0.2 copy.156
  106.2 0.4 multiply_reduce_fusion
  106.9 0.7 copy.109
  107.6 0.4 reshape.156
  108.0 0.5 convolution_convert_fusion
  108.7 0.3 copy.120
  108.9 1.0 copy.121
  109.9 0.5 convolution_convert_fusion.1
  110.5 1.0 copy.117
  111.5 4.8 %fusion.74 = (f32[8,8,128]{2,1,0:T(8,128)S(1)}, f32[8,8,128,128]{2,3,1,0:T(8,128)}) fusion(pred[8,128]{1,0:T(8,128)(4,1)S(1)} %copy.119, bf16[128,8,8,32]{0,3,2,1:T(8,128)(2,1)S(1)} %bitcast.155, bf16[128,8,8,32]{0,3,2,1:T(8,128)(2,1)} %bitcast.156), kind=kOutput, calls=%fused_computation.114 | convolution fusion | flops 71303296 | bytes 5276672 | tf_op jit(solution)/shard_map/sub | solution.py:56
  116.3 3.0 %fusion.17 = f32[8,8,32,128]{3,2,1,0:T(8,128)S(1)} fusion(bf16[128,8,8,32]{0,3,2,1:T(8,128)(2,1)} %bitcast.157, f32[8,8,128,128]{2,3,1,0:T(8,128)} %get-tuple-element.66, f32[8,8,128]{2,1,0:T(8,128)S(1)} %get-tuple-element.65), kind=kOutput, calls=%fused_computation.26 | convolution fusion | flops 69206016 | bytes 5799936 | tf_op jit(solution)/shard_map/rhst,trhd->srhd/dot_general | solution.py:57
  119.4 1.3 copy.123
  120.7 1.7 fusion.20
  122.4 0.3 copy.124
  122.7 18.4 %all_to_all.64 = bf16[128,8,256]{2,1,0:T(8,128)(2,1)S(1)} all-to-all(bf16[128,8,256]{2,1,0:T(8,128)(2,1)S(1)} %copy.124), channel_id=1, replica_groups=mesh['dp'=1,'dap'=32] {'dap'}, dimensions={0} | all-to-all | bytes 1048576 | tf_op jit(solution)/shard_map/all_to_all | solution.py:125
  141.1 0.4 convert_reduce_fusion.2
  141.4 0.2 copy.158
  142.0 0.7 fusion.34
  143.0 0.3 copy.157
  143.4 0.5 fusion.25
  143.9 0.6 fusion.71
  144.7 39.2 %all-gather = bf16[32,4,256]{2,1,0:T(4,128)(2,1)S(1)} all-gather(bf16[1,4,256]{2,1,0:T(4,128)(2,1)S(1)} %bitcast.162), channel_id=1, replica_groups=mesh['dp'=1,'dap'=32] {'dap'}, dimensions={0}, use_global_device_ids=true | all-gather | bytes 67584 | tf_op jit(solution)/shard_map/all_gather | solution.py:131
  183.9 0.2 copy.133
  184.1 0.8 reshape.172
  185.0 2.8 %all-to-all-start.3 = ((bf16[32,2,512]{2,1,0:T(2,128)(2,1)}), bf16[32,2,512]{2,1,0:T(2,128)(2,1)S(1)}, u32[]{:S(2)}, u32[]{:S(2)}) async-start(bf16[32,2,512]{2,1,0:T(2,128)(2,1)} %reshape.172), calls=%async_computation.3 | async-start | bytes 131072 | tf_op jit(solution)/shard_map/all_to_all | solution.py:128
  187.9 7.5 %all-to-all-done.3 = bf16[32,2,512]{2,1,0:T(2,128)(2,1)S(1)} async-done(((bf16[32,2,512]{2,1,0:T(2,128)(2,1)}), bf16[32,2,512]{2,1,0:T(2,128)(2,1)S(1)}, u32[]{:S(2)}, u32[]{:S(2)}) %all-to-all-start.3) | async-done | bytes 65568 | tf_op jit(solution)/shard_map/all_to_all | solution.py:128
  195.4 0.2 reshape.173
  195.7 0.2 copy.136
  195.9 3.8 %all-gather.6.cloned.1.call-done = bf16[128,256,32]{1,2,0:T(8,128)(2,1)} async-done(((bf16[4,256,32]{1,2,0:T(8,128)(2,1)}), bf16[128,256,32]{1,2,0:T(8,128)(2,1)}) %all-gather.6.cloned.1.call-update) | async-done | bytes 2097168 | tf_op jit(solution)/shard_map/all_gather | solution.py:130
  199.7 4.0 %reshape.154 = bf16[128,2,128,32]{2,1,3,0:T(2,128)(2,1)} reshape(bf16[128,256,32]{1,2,0:T(8,128)(2,1)} %all-gather.6.cloned.1.call-done) | data formatting | bytes 4194304 | tf_op jit(solution)/shard_map/reshape | solution.py:140
  203.7 2.9 %copy.155 = bf16[128,2,128,32]{2,0,3,1:T(8,128)(2,1)S(1)} copy(bf16[128,2,128,32]{2,1,3,0:T(2,128)(2,1)} %reshape.154) | data formatting | bytes 4194304 | tf_op jit(solution)/shard_map/reshape | solution.py:140
  206.6 7.3 %while.10 = (s32[]{:T(128)}, f32[2,8,128,128]{3,2,1,0:T(8,128)}, bf16[2,128,128,32]{2,1,3,0:T(8,128)(2,1)S(1)}, bf16[128,8,32]{0,2,1:T(8,128)(2,1)S(1)}, bf16[1024,128]{1,0:T(8,128)(2,1)S(1)}, /*index=5*/s32[]{:T(128)}) while((s32[]{:T(128)}, f32[2,8,128,128]{3,2,1,0:T(8,128)}, bf16[2,128,128,32]{2,1,3,0:T(8,128)(2,1)S(1)}, ...), condition=%wide.region_13.14_spmd, body=%wide.region_12.13_spmd.sunk | while | flops 537919488 | bytes 10289737 | solution.py:150
  206.6 0.7 convert_bitcast_fusion.2
  207.3 1.4 copy.161
  208.7 1.6 fusion.97
  210.3 0.7 convert_bitcast_fusion.2
  211.0 1.4 copy.161
  212.3 1.6 fusion.97
  213.9 1.3 copy.137
  215.2 1.2 fusion.35
  (74 shorter events, 2.4 us)
Async XLA Ops:
  7.2 17.1 %copy-start = (bf16[256,512]{1,0:T(8,128)(2,1)S(1)}, bf16[256,512]{1,0:T(8,128)(2,1)}, u32[]{:S(2)}) copy-start(bf16[256,512]{1,0:T(8,128)(2,1)} %param.26) | copy-start | bytes 786436
  7.2 62.1 %all-gather.4.cloned.1.call-start = ((), (), s32[]{:S(2)}) async-start(), calls=%async_computation.4 | async-start | bytes 1081344 | tf_op jit(solution)/shard_map/all_gather | solution.py:103
  10.2 16.9 %copy-start.10 = (s32[256]{0:T(256)S(1)}, s32[256]{0:T(256)}, u32[]{:S(2)}) copy-start(s32[256]{0:T(256)} %param.22) | copy-start | bytes 3076
  10.2 16.9 %copy-start.3 = (bf16[4,256,256]{2,1,0:T(8,128)(2,1)S(1)}, bf16[4,256,256]{2,1,0:T(8,128)(2,1)}, u32[]{:S(2)}) copy-start(bf16[4,256,256]{2,1,0:T(8,128)(2,1)} %param.19) | copy-start | bytes 1572868
  10.2 16.9 %copy-start.11 = (bf16[256,512]{1,0:T(8,128)(2,1)S(1)}, bf16[256,512]{1,0:T(8,128)(2,1)}, u32[]{:S(2)}) copy-start(bf16[256,512]{1,0:T(8,128)(2,1)} %param.27) | copy-start | bytes 786436
  10.3 16.9 %copy-start.14 = (f32[256]{0:T(256)S(1)}, f32[256]{0:T(256)}, u32[]{:S(2)}) copy-start(f32[256]{0:T(256)} %param.23) | copy-start | bytes 3076
  14.2 72.0 %all-to-all-start.1 = ((bf16[4,32,8]{2,0,1:T(4,128)(2,1)}), bf16[4,32,8]{2,0,1:T(4,128)(2,1)S(1)}, u32[]{:S(2)}, u32[]{:S(2)}) async-start(bf16[4,32,8]{2,0,1:T(4,128)(2,1)} %copy.118), calls=%async_computation.1 | async-start | bytes 65536 | tf_op jit(solution)/shard_map/all_to_all | solution.py:109
  25.8 3.0 %copy-start.8 = (s32[4,256]{1,0:T(4,128)S(1)}, s32[4,256]{1,0:T(4,128)}, u32[]{:S(2)}) copy-start(s32[4,256]{1,0:T(4,128)} %param.21) | copy-start | bytes 12292
  27.6 1.2 copy-start.7
  78.8 4.8 %copy-start.12 = (bf16[256,256]{1,0:T(8,128)(2,1)S(1)}, bf16[256,256]{1,0:T(8,128)(2,1)}, u32[]{:S(2)}) copy-start(bf16[256,256]{1,0:T(8,128)(2,1)} %param.28) | copy-start | bytes 393220
  86.2 19.1 %all-to-all-start = ((bf16[4,256,256]{2,0,1:T(4,128)(2,1)}), bf16[4,256,256]{2,0,1:T(4,128)(2,1)S(1)}, u32[]{:S(2)}, u32[]{:S(2)}) async-start(bf16[4,256,256]{2,0,1:T(4,128)(2,1)} %copy.107), calls=%async_computation | async-start | bytes 1048576 | tf_op jit(solution)/shard_map/all_to_all | solution.py:108
  89.8 109.9 %all-gather.6.cloned.1.call-start = ((), (), s32[]{:S(2)}) async-start(), calls=%async_computation.5 | async-start | bytes 2162688 | tf_op jit(solution)/shard_map/all_gather | solution.py:130
  105.7 2.3 %copy-start.5 = (bf16[256,512]{1,0:T(8,128)(2,1)S(1)}, bf16[256,512]{1,0:T(8,128)(2,1)}, u32[]{:S(2)}) copy-start(bf16[256,512]{1,0:T(8,128)(2,1)} %param.30) | copy-start | bytes 786436
  105.7 2.3 %copy-start.9 = (f32[256]{0:T(256)S(1)}, f32[256]{0:T(256)}, u32[]{:S(2)}) copy-start(f32[256]{0:T(256)} %param.29) | copy-start | bytes 3076
  107.6 2.4 %copy-start.6 = (bf16[256,512]{1,0:T(8,128)(2,1)S(1)}, bf16[256,512]{1,0:T(8,128)(2,1)}, u32[]{:S(2)}) copy-start(bf16[256,512]{1,0:T(8,128)(2,1)} %param.31) | copy-start | bytes 786436
  122.3 21.1 %copy-start.13 = (bf16[256,64]{0,1:T(8,128)(2,1)S(1)}, bf16[256,64]{0,1:T(8,128)(2,1)}, u32[]{:S(2)}) copy-start(bf16[256,64]{0,1:T(8,128)(2,1)} %param.34) | copy-start | bytes 98308
  122.3 21.1 %copy-start.15 = (f32[256]{0:T(256)S(1)}, f32[256]{0:T(256)}, u32[]{:S(2)}) copy-start(f32[256]{0:T(256)} %param.33) | copy-start | bytes 3076
  143.3 52.4 %copy-start.4 = (bf16[4,32,8,256]{3,2,1,0:T(8,128)(2,1)}, bf16[4,32,8,256]{3,2,1,0:T(8,128)(2,1)S(1)}, u32[]{:S(2)}) copy-start(bf16[4,32,8,256]{3,2,1,0:T(8,128)(2,1)S(1)} %copy.157) | copy-start | bytes 1572868
  185.0 10.4 %all-to-all-start.3 = ((bf16[32,2,512]{2,1,0:T(2,128)(2,1)}), bf16[32,2,512]{2,1,0:T(2,128)(2,1)S(1)}, u32[]{:S(2)}, u32[]{:S(2)}) async-start(bf16[32,2,512]{2,1,0:T(2,128)(2,1)} %reshape.172), calls=%async_computation.3 | async-start | bytes 131072 | tf_op jit(solution)/shard_map/all_to_all | solution.py:128
  195.9 10.7 %copy-start.1 = (bf16[1024,128]{1,0:T(8,128)(2,1)S(1)}, bf16[1024,128]{1,0:T(8,128)(2,1)}, u32[]{:S(2)}) copy-start(bf16[1024,128]{1,0:T(8,128)(2,1)} %param.35) | copy-start | bytes 786436
  206.6 8.6 %copy-start.2 = (bf16[8,256,128]{2,1,0:T(8,128)(2,1)S(1)}, bf16[8,256,128]{2,1,0:T(8,128)(2,1)}, u32[]{:S(2)}) copy-start(bf16[8,256,128]{2,1,0:T(8,128)(2,1)} %param.20) | copy-start | bytes 1572868
Sparse Core Ops, SparseCore 0:
  12.9 56.3 all-gather.3
  144.7 54.9 all-gather.5
where the time goes:
time: 224 us; the launch traced here: 223 us
  waiting for transfers between devices  67 us (30%)
  blocking collectives  57.6 us (26%)
  matrix products  33.7 us (15%)
  local copies, waits for them, and re-layouts  26.9 us (12%)
  between operations  14.6 us (7%)
  starting transfers between devices  13.9 us (6%)
  other arithmetic  9.53 us (4%)
    all_gather x1, waiting for transfers between devices, body(): lax.all_gather(pair_bias, 'dap', axis=1, tiled=True).astype(jnp.float32)  40.5 us
    all_gather x1, blocking collectives, body(): lax.all_gather(mask_narrow, 'dap', axis=0, tiled=True)  39.2 us
    all_to_all x1, blocking collectives, body(): lax.all_to_all(second_update, 'dap', split_axis=0, concat_axis=1, tiled=T...  18.4 us
    all_to_all x1, waiting for transfers between devices, body(): lax.all_to_all(first_update, 'dap', split_axis=1, concat_axis=0, tiled=True)  15.2 us
    dot_general x9, matrix products, linear(): jnp.einsum('...c,cd->...d', inputs, weight, preferred_element_type=jnp.fl...  9.78 us
    sub x1, matrix products, row_attend(): weights = jax.nn.softmax(scores, axis=-1).astype(jnp.bfloat16)  7.63 us
    all_to_all x1, waiting for transfers between devices, body(): lax.all_to_all(sides[..., :C_OPM], 'dap', split_axis=1, concat_axis=0, ti...  7.48 us
    all_to_all x1, starting transfers between devices, body(): lax.all_to_all(mask_narrow, 'dap', split_axis=1, concat_axis=0, tiled=True)  7.3 us
  transfers between devices with their start and end apart: 5, of which 4 were waited for; matrix products, arithmetic and copies ran while one was open for 12% of the time, Pallas kernels for 0%

commit v1 on v0

v1 whole, which is shorter than its diff:
```python
import functools
import math

import jax
import jax.numpy as jnp
from jax import lax
from jax.experimental import pallas as pl
from jax.experimental.pallas import tpu as pltpu
from jax.sharding import PartitionSpec as P

HEADS = 8
HEAD = 32
C_OPM = 32
LOG2E = math.log2(math.e)
SCALE = LOG2E / math.sqrt(HEAD)
MASKED = -1000000000.0 * LOG2E
NT = (((1,), (1,)), ((), ()))
MESH = pl.DeviceIdType.MESH
VMEM = pl.BlockSpec(memory_space=pltpu.VMEM)
LIMIT = 48 * 1024 * 1024


def norm(wide, gain):
    average = jnp.mean(wide, axis=-1, keepdims=True)
    centred = wide - average
    spread = jnp.mean(centred * centred, axis=-1, keepdims=True)
    return (centred * lax.rsqrt(spread + 1e-05) * gain).astype(jnp.bfloat16)


def dot(a, b):
    return jnp.dot(a, b, preferred_element_type=jnp.float32)


def dot_nt(a, b):
    return lax.dot_general(a, b, NT, preferred_element_type=jnp.float32)


def greet(partners):
    barrier = pltpu.get_barrier_semaphore()
    for partner in partners:
        pl.semaphore_signal(barrier, inc=1, device_id={"dap": partner}, device_id_type=MESH)
    pl.semaphore_wait(barrier, len(partners))


def greet_all(n, me):
    barrier = pltpu.get_barrier_semaphore()

    def one(k, carry):
        pl.semaphore_signal(
            barrier, inc=1, device_id={"dap": lax.rem(me + k, n)}, device_id_type=MESH
        )
        return carry

    lax.fori_loop(1, n, one, 0)
    pl.semaphore_wait(barrier, n - 1)


class Gather:
    def __init__(self, n, me, out, zs, zr, ps, pr, cs, cr):
        self.n, self.me, self.out = n, me, out
        self.sems = {"z": (zs, zr), "p": (ps, pr), "c": (cs, cr)}
        self.layers = n // 8
        self.z = me // 8
        self.p = lax.rem(me // 2, 4)
        self.c = lax.rem(me, 2)

    def place(self, z, p, c):
        return z * 8 + p * 2 + c

    def plane(self, p, k):
        if k == 0:
            return p
        if k == 1:
            return p + 1 - 2 * lax.rem(p, 2)
        if k == 2:
            return lax.rem(p + 2, 4)
        return 3 - p

    def partners(self):
        found = [self.place(lax.rem(self.z + d, self.layers), self.p, self.c) for d in range(1, self.layers)]
        found += [self.place(self.z, self.plane(self.p, k), self.c) for k in (1, 2, 3)]
        return found + [self.place(self.z, self.p, 1 - self.c)]

    def copy(self, kind, slot, block, target):
        send, recv = self.sems[kind]
        return pltpu.make_async_remote_copy(
            src_ref=self.out.at[block],
            dst_ref=self.out.at[block],
            send_sem=send.at[slot],
            recv_sem=recv.at[slot],
            device_id={"dap": target},
            device_id_type=MESH,
        )

    def layer(self, d):
        return lax.rem(self.z + self.layers - d, self.layers)

    def z_copy(self, d):
        return self.copy("z", d, self.me, self.place(lax.rem(self.z + d, self.layers), self.p, self.c))

    def p_copy(self, d, k):
        block = self.place(self.layer(d), self.p, self.c)
        return self.copy("p", d * 4 + k, block, self.place(self.z, self.plane(self.p, k), self.c))

    def c_copy(self, d, k):
        block = self.place(self.layer(d), self.plane(self.p, k), self.c)
        return self.copy("c", d * 4 + k, block, self.place(self.z, self.p, 1 - self.c))

    def z_arrived(self, d):
        block = self.place(self.layer(d), self.p, self.c)
        self.copy("z", d, block, self.place(lax.rem(self.z + d, self.layers), self.p, self.c)).wait_recv()

    def p_arrived(self, d, k):
        block = self.place(self.layer(d), self.plane(self.p, k), self.c)
        self.copy("p", d * 4 + k, block, self.place(self.z, self.plane(self.p, k), self.c)).wait_recv()

    def c_arrived(self, d, k):
        block = self.place(self.layer(d), self.plane(self.p, k), 1 - self.c)
        self.copy("c", d * 4 + k, block, self.place(self.z, self.p, 1 - self.c)).wait_recv()

    def start(self):
        for d in range(1, self.layers):
            self.z_copy(d).start()
        for k in (1, 2, 3):
            self.p_copy(0, k).start()
        self.c_copy(0, 0).start()

    def relay(self):
        for d in range(1, self.layers):
            self.z_arrived(d)
            for k in (1, 2, 3):
                self.p_copy(d, k).start()
            self.c_copy(d, 0).start()
        for d in range(self.layers):
            for k in (1, 2, 3):
                self.p_arrived(d, k)
                self.c_copy(d, k).start()

    def finish(self):
        for d in range(self.layers):
            for k in range(4):
                self.c_arrived(d, k)
        for d in range(self.layers):
            if d > 0:
                self.z_copy(d).wait_send()
            for k in range(4):
                if k > 0:
                    self.p_copy(d, k).wait_send()
                self.c_copy(d, k).wait_send()


def gather_sems(n):
    layers = n // 8
    sizes = (layers, layers, layers * 4, layers * 4, layers * 4, layers * 4)
    return [pltpu.SemaphoreType.DMA((size,)) for size in sizes]


class Exchange:
    def __init__(self, n, me, src, dst, send, recv):
        self.n, self.me, self.src, self.dst, self.send, self.recv = n, me, src, dst, send, recv

    def copy(self, k, block_out, block_in):
        return pltpu.make_async_remote_copy(
            src_ref=self.src.at[block_out],
            dst_ref=self.dst.at[block_in],
            send_sem=self.send.at[k],
            recv_sem=self.recv.at[k],
            device_id={"dap": block_out},
            device_id_type=MESH,
        )

    def start(self):
        def one(k, carry):
            self.copy(k, lax.rem(self.me + k, self.n), self.me).start()
            return carry

        lax.fori_loop(1, self.n, one, 0)

    def finish(self):
        def one(k, carry):
            target = lax.rem(self.me + k, self.n)
            self.copy(k, target, lax.rem(self.me + self.n - k, self.n)).wait_recv()
            self.copy(k, target, self.me).wait_send()
            return carry

        lax.fori_loop(1, self.n, one, 0)


def bias_kernel(n, pair_ref, gain_ref, weight_ref, out_ref, turned, *sems):
    me = lax.axis_index("dap")
    gather = Gather(n, me, out_ref, *sems)
    rows = pair_ref.shape[0]
    for i in range(rows):
        normed = norm(pair_ref[i].astype(jnp.float32), gain_ref[...])
        turned[:, i, :] = dot_nt(weight_ref[...], normed)
    out_ref[me] = turned[...].reshape(out_ref.shape[1:]).astype(jnp.bfloat16)
    greet(gather.partners())
    gather.start()
    gather.relay()
    gather.finish()


def attend(joint, gated, keep, width, bias):
    queries, keys_all = joint[:, :width], joint[:, width:]
    values_all, gates = gated[:, :width], gated[:, width:]
    lanes = lax.broadcasted_iota(jnp.int32, (1, width), 1) // HEAD
    total = None
    for h in range(HEADS):
        mine = (lanes == h).astype(jnp.float32).astype(jnp.bfloat16)
        scores = dot_nt(queries * mine, keys_all) * SCALE
        if bias is not None:
            scores = scores + bias(h)
        scores = jnp.where(keep, scores, MASKED)
        powers = jnp.exp2(scores - jnp.max(scores, axis=-1, keepdims=True))
        weights = powers * (1.0 / jnp.sum(powers, axis=-1, keepdims=True))
        part = dot(weights.astype(jnp.bfloat16), values_all * mine)
        total = part if total is None else total + part
    return (total * jax.nn.sigmoid(gates.astype(jnp.float32))).astype(jnp.bfloat16)


def row_kernel(al_ref, bias_ref, keep_ref, gain_ref, scoring_ref, values_ref, output_ref, out_ref, wide):
    @pl.when(pl.program_id(0) == 0)
    def _():
        wide[...] = bias_ref[...].astype(jnp.float32) * LOG2E

    length, width = al_ref.shape[1:]
    stream = al_ref[0].astype(jnp.float32)
    normed = norm(stream, gain_ref[...])
    joint = dot(normed, scoring_ref[...]).astype(jnp.bfloat16)
    gated = dot(normed, values_ref[...]).astype(jnp.bfloat16)
    span = wide.shape[1] // HEADS

    def bias(h):
        return wide[:, h * span : (h + 1) * span, :].reshape(length, length)

    mixed = attend(joint, gated, keep_ref[0] > 0, width, bias)
    out_ref[0] = (stream + dot(mixed, output_ref[...])).astype(jnp.bfloat16)


def swap_kernel(n, src_ref, out_ref, send, recv):
    me = lax.axis_index("dap")
    exchange = Exchange(n, me, src_ref, out_ref, send, recv)
    greet_all(n, me)
    exchange.start()
    out_ref[me] = src_ref[me]
    exchange.finish()


def column_kernel(
    in_ref, keep_ref, gain_ref, scoring_ref, values_ref, output_ref, outer_gain_ref, sides_ref,
    new_ref, left_ref, right_ref, wide, turned,
):
    i = pl.program_id(0)
    rows, width = wide.shape[1:]

    @pl.when(i == 0)
    def _():
        wide[...] = in_ref[...].astype(jnp.float32).reshape(wide.shape)

    stream = wide[:, i, :]
    normed = norm(stream, gain_ref[...])
    joint = dot(normed, scoring_ref[...]).astype(jnp.bfloat16)
    gated = dot(normed, values_ref[...]).astype(jnp.bfloat16)
    keep = keep_ref[0]
    mixed = attend(joint, gated, keep > 0, width, None)
    second = (stream + dot(mixed, output_ref[...])).astype(jnp.bfloat16).astype(jnp.float32)
    wide[:, i, :] = second
    sides = dot_nt(sides_ref[...], norm(second, outer_gain_ref[...])) * keep
    left_ref[0] = sides[:C_OPM].astype(jnp.bfloat16)
    turned[:, i, :] = sides[C_OPM:]

    @pl.when(i == rows - 1)
    def _():
        new_ref[...] = wide[...].reshape(new_ref.shape).astype(jnp.bfloat16)
        right_ref[...] = turned[...].reshape(right_ref.shape).astype(jnp.bfloat16)


def spread_kernel(n, new_ref, right_ref, new_out, right_out, send, recv, *sems):
    me = lax.axis_index("dap")
    gather = Gather(n, me, right_out, *sems)
    exchange = Exchange(n, me, new_ref, new_out, send, recv)
    right_out[me] = right_ref[...]
    greet_all(n, me)
    gather.start()
    exchange.start()
    new_out[me] = new_ref[me]
    gather.relay()
    gather.finish()
    exchange.finish()


def outer_kernel(left_ref, right_ref, weight_ref, scale_ref, pair_ref, out_ref, wide, products):
    rows = pair_ref.shape[0]
    total = pair_ref.shape[1]
    span = wide.shape[1] // C_OPM
    left = left_ref[...].reshape(rows * C_OPM, left_ref.shape[2])
    wide[...] = right_ref[...].astype(jnp.float32)
    for e in range(C_OPM):
        piece = wide[:, e * span : (e + 1) * span, :].reshape(total, wide.shape[2])
        block = dot_nt(left, piece.astype(jnp.bfloat16)).astype(jnp.bfloat16)
        products[:, e * C_OPM : (e + 1) * C_OPM, :] = block.reshape(rows, C_OPM, total)
    for i in range(rows):
        flat = dot(weight_ref[...], products[i]) * scale_ref[i : i + 1, :]
        out_ref[i] = (pair_ref[i].astype(jnp.float32) + flat.T).astype(jnp.bfloat16)


def body(
    n,
    alignment,
    pair_rep,
    align_mask,
    residue_mask,
    row_gain,
    pair_gain,
    row_bias,
    row_scoring,
    row_values,
    row_output,
    column_gain,
    column_scoring,
    column_values,
    column_output,
    outer_gain,
    outer_inputs,
    outer_output,
):
    seqs, total_res, width = alignment.shape
    rows, _, channels = pair_rep.shape
    total_seqs = seqs * n
    narrow, wide = jnp.bfloat16, jnp.float32
    shape = jax.ShapeDtypeStruct
    me = lax.axis_index("dap")

    every_mask = lax.all_gather(align_mask, "dap", axis=0, tiled=True).astype(wide)
    residue_float = residue_mask.astype(wide)
    keep_rows = (align_mask.astype(wide) * residue_float[None, :])[:, None, :]
    keep_columns = lax.dynamic_slice_in_dim(every_mask, me * rows, rows, 1).T
    row_factor = lax.dynamic_slice_in_dim(residue_float, me * rows, rows)
    pair_count = jnp.dot(keep_columns, every_mask)
    scale = row_factor[:, None] * residue_float[None, :] / (0.001 + pair_count)
    turned_output = outer_output.reshape(C_OPM, C_OPM, channels).transpose(2, 1, 0).reshape(channels, -1)

    def params(**more):
        return pltpu.CompilerParams(vmem_limit_bytes=LIMIT, **more)

    every_bias = pl.pallas_call(
        functools.partial(bias_kernel, n),
        out_shape=shape((n, HEADS * rows, total_res), narrow),
        in_specs=[VMEM] * 3,
        out_specs=VMEM,
        scratch_shapes=[pltpu.VMEM((HEADS, rows, total_res), wide)] + gather_sems(n),
        compiler_params=params(collective_id=0, has_side_effects=True),
        name="bias_gather",
    )(pair_rep, pair_gain[None], row_bias.T)

    def whole(array):
        return pl.BlockSpec(array.shape, lambda i: (0,) * array.ndim)

    def one(*tail):
        return pl.BlockSpec((1,) + tail, lambda i: (i, 0, 0))

    first_update = pl.pallas_call(
        row_kernel,
        out_shape=shape(alignment.shape, narrow),
        grid=(seqs,),
        in_specs=[
            one(total_res, width), whole(every_bias), one(1, total_res), whole(row_gain[None]),
            whole(row_scoring), whole(row_values), whole(row_output),
        ],
        out_specs=one(total_res, width),
        scratch_shapes=[pltpu.VMEM(every_bias.shape, wide)],
        compiler_params=params(),
        name="row_attention",
    )(alignment, every_bias, keep_rows, row_gain[None], row_scoring, row_values, row_output)

    blocks = jnp.swapaxes(first_update.reshape(seqs, n, rows, width), 0, 1).reshape(n, seqs * rows, width)
    columns = pl.pallas_call(
        functools.partial(swap_kernel, n),
        out_shape=shape(blocks.shape, narrow),
        in_specs=[VMEM],
        out_specs=VMEM,
        scratch_shapes=[pltpu.SemaphoreType.DMA((n,)), pltpu.SemaphoreType.DMA((n,))],
        compiler_params=params(collective_id=1, has_side_effects=True),
        name="to_columns",
    )(blocks)

    turned_inputs = outer_inputs.T
    right_shape = (C_OPM * rows, total_seqs)
    new_blocks, left, right = pl.pallas_call(
        column_kernel,
        out_shape=(
            shape(blocks.shape, narrow),
            shape((rows, C_OPM, total_seqs), narrow),
            shape(right_shape, narrow),
        ),
        grid=(rows,),
        in_specs=[
            whole(columns), one(1, total_seqs), whole(column_gain[None]), whole(column_scoring),
            whole(column_values), whole(column_output), whole(outer_gain[None]), whole(turned_inputs),
        ],
        out_specs=(
            pl.BlockSpec(blocks.shape, lambda i: (0, 0, 0)),
            one(C_OPM, total_seqs),
            pl.BlockSpec(right_shape, lambda i: (0, 0)),
        ),
        scratch_shapes=[
            pltpu.VMEM((total_seqs, rows, width), wide),
            pltpu.VMEM((C_OPM, rows, total_seqs), wide),
        ],
        compiler_params=params(),
        name="column_attention",
    )(
        columns, keep_columns[:, None, :], column_gain[None], column_scoring, column_values,
        column_output, outer_gain[None], turned_inputs,
    )

    new_back, every_right = pl.pallas_call(
        functools.partial(spread_kernel, n),
        out_shape=(shape(blocks.shape, narrow), shape((n,) + right_shape, narrow)),
        in_specs=[VMEM] * 2,
        out_specs=(VMEM, VMEM),
        scratch_shapes=[pltpu.SemaphoreType.DMA((n,)), pltpu.SemaphoreType.DMA((n,))] + gather_sems(n),
        compiler_params=params(collective_id=2, has_side_effects=True),
        name="spread",
    )(new_blocks, right)

    new_pair = pl.pallas_call(
        outer_kernel,
        out_shape=shape(pair_rep.shape, narrow),
        in_specs=[VMEM] * 5,
        out_specs=VMEM,
        scratch_shapes=[
            pltpu.VMEM((n,) + right_shape, wide),
            pltpu.VMEM((rows, C_OPM * C_OPM, total_res), narrow),
        ],
        compiler_params=params(),
        name="outer_product",
    )(left, every_right, turned_output, scale, pair_rep)
    new_alignment = jnp.swapaxes(new_back.reshape(n, seqs, rows, width), 0, 1).reshape(alignment.shape)
    return new_alignment, new_pair


def solution(mesh):
    split = P(("dp", "dap"), None, None)
    in_specs = (split, split, P(("dp", "dap"), None), P("dp")) + (P(),) * 13
    return jax.shard_map(
        functools.partial(body, mesh.shape["dap"]),
        mesh=mesh,
        in_specs=in_specs,
        out_specs=(split, split),
        check_vma=False,
    )
```

time: 224 us -> 135 us (0.60)
  Pallas kernels: 0 us -> 78.7 us
  waiting for transfers between devices: 67 us -> 0 us
  matrix products: 33.7 us -> 0.17 us
  local copies, waits for them, and re-layouts: 26.9 us -> 9.31 us
  starting transfers between devices: 13.9 us -> 0 us
  blocking collectives: 57.6 us -> 43.7 us
  between operations: 14.6 us -> 0.82 us
  other arithmetic: 9.53 us -> 1.4 us
    pallas_call x0 -> x6, Pallas kernels: none -> 78.7 us  [the longest x1 24 us: body(): pl.pallas_call(functools.partial(spread_kernel, n), out_shape=(shape(bloc...]
    all_gather x2 -> x0, waiting for transfers between devices: 44.3 us -> none  [the longest x1 40.5 us: body(): lax.all_gather(pair_bias, 'dap', axis=1, tiled=True).astype(jnp.float32)]
    all_to_all x3 -> x0, waiting for transfers between devices: 22.7 us -> none  [the longest x1 15.2 us: body(): lax.all_to_all(first_update, 'dap', split_axis=1, concat_axis=0, tiled=True)]
    dot_general x15 -> x1, matrix products: 21.3 us -> 0.17 us  [body(): pair_count = jnp.dot(keep_columns, every_mask)]
    all_to_all x1 -> x0, blocking collectives: 18.4 us -> none  [body(): lax.all_to_all(second_update, 'dap', split_axis=0, concat_axis=1, tiled=T...]
    all_to_all x3 -> x0, starting transfers between devices: 13.7 us -> none  [the longest x1 7.3 us: body(): lax.all_to_all(mask_narrow, 'dap', split_axis=1, concat_axis=0, tiled=True)]
    sub x2 -> x0, matrix products: 12.5 us -> none  [the longest x1 7.63 us: row_attend(): weights = jax.nn.softmax(scores, axis=-1).astype(jnp.bfloat16)]
    reshape x4 -> x3, local copies, waits for them, and re-layouts: 8.59 us -> 1.03 us  [the longest x1 0.83 us: body(): jnp.swapaxes(new_back.reshape(n, seqs, rows, width), 0, 1)]
  transfers between devices with their start and end apart: 5 -> 0, of which waited for: 4 -> 0; matrix products, arithmetic and copies ran while one was open for 12% -> 0% of each run, Pallas kernels for 0% -> 0%
where the time goes in v1:
time: 135 us; the launch traced here: 134 us
  Pallas kernels  78.7 us (58%)
  blocking collectives  43.7 us (32%)
  local copies, waits for them, and re-layouts  9.31 us (7%)
  other arithmetic  1.4 us (1%)
    all_gather x1, blocking collectives, body(): lax.all_gather(align_mask, 'dap', axis=0, tiled=True).astype(wide)  43.7 us
    pallas_call x1, Pallas kernels, body(): pl.pallas_call(functools.partial(spread_kernel, n), out_shape=(shape(bloc...  24 us
    pallas_call x1, Pallas kernels, body(): pl.pallas_call(functools.partial(bias_kernel, n), out_shape=shape((n, HEA...  16.7 us
    pallas_call x1, Pallas kernels, body(): pl.pallas_call(column_kernel, out_shape=(shape(blocks.shape, narrow), sha...  13.7 us
    pallas_call x1, Pallas kernels, body(): pl.pallas_call(functools.partial(swap_kernel, n), out_shape=shape(blocks....  13.5 us
    pallas_call x1, Pallas kernels, body(): pl.pallas_call(row_kernel, out_shape=shape(alignment.shape, narrow), grid...  8.16 us
    unnamed x34, local copies, waits for them, and re-layouts  7.09 us
    pallas_call x1, Pallas kernels, body(): pl.pallas_call(outer_kernel, out_shape=shape(pair_rep.shape, narrow), in_...  2.73 us

profile of v1, /device:TPU:0, one launch (start us, length us, event | category | flops | bytes accessed | tf_op | source)
XLA Modules:
  0.0 134.1 jit_solution(17747361536554575480)
XLA Ops:
  0.6 0.0 copy-start
  0.6 1.0 copy-done
  1.7 0.0 copy-start.10
  1.7 0.7 copy-done.10
  2.4 0.0 copy-start.14
  2.4 0.7 copy-done.14
  3.0 16.7 %bias_gather.1.bias_ref = bf16[32,64,256]{2,1,0:T(8,128)(2,1)S(1)} custom-call(bf16[8,256,128]{2,1,0:T(8,128)(2,1)S(1)} %copy-done, f32[1,128]{1,0:T(1,128)S(1)} %bitcast.36, bf16[8,128]{1,0:T(8,128)(2,1)S(1)} %bitcast.32), custom_call_target="tpu_custom_call" | custom-call | tf_op jit(solution)/shard_map/bias_gather/pallas_call | solution.py:346
  19.7 0.7 convert_element_type.10
  20.4 0.7 convert_multiply_fusion
  21.1 0.0 copy-start.2
  21.1 1.0 copy-done.2
  22.1 0.0 copy-start.3
  22.1 0.9 copy-done.3
  23.1 0.0 copy-start.4
  23.1 0.9 copy-done.4
  24.0 0.0 copy-start.7
  24.0 0.9 copy-done.7
  24.9 0.0 copy-start.11
  24.9 0.7 copy-done.11
  25.6 0.0 copy-start.15
  25.6 8.2 %row_attention.1 = bf16[4,256,256]{2,1,0:T(8,128)(2,1)S(1)} custom-call(bf16[4,256,256]{2,1,0:T(8,128)(2,1)S(1)} %copy-done.2, bf16[32,64,256]{2,1,0:T(8,128)(2,1)S(1)} %bias_gather.1.bias_ref, f32[4,1,256]{2,1,0:T(1,128)S(1)} %broadcast_in_dim.22.keep_ref, f32[1,256]{1,0:T(1,128)S(1)} %bitcast.33, bf16[256,512]{1,0:T(8,128)(2,1)S(1)} %copy-done.3, ...), custom_call_target="tpu_custom_call" | custom-call | tf_op jit(solution)/shard_map/row_attention/pallas_call | solution.py:362
  33.8 0.0 copy-start.5
  33.8 0.0 copy-start.6
  33.8 0.0 copy-start.8
  33.8 0.0 copy-start.9
  33.8 0.0 copy-start.12
  33.8 0.0 copy-start.13
  33.8 0.1 copy_bitcast_fusion.1.src_ref
  33.9 13.5 %to_columns.1.in_ref = bf16[32,32,256]{2,1,0:T(8,128)(2,1)S(1)} custom-call(bf16[32,32,256]{2,1,0:T(8,128)(2,1)S(1)} %copy_bitcast_fusion.1.src_ref), custom_call_target="tpu_custom_call" | custom-call | tf_op jit(solution)/shard_map/to_columns/pallas_call | solution.py:377
  47.4 0.0 copy-done.15
  47.4 43.7 %all-gather = s32[32,4,256]{2,1,0:T(4,128)S(1)} all-gather(s32[1,4,256]{2,1,0:T(4,128)S(1)} %bitcast.39), channel_id=1, replica_groups=mesh['dp'=1,'dap'=32] {'dap'}, dimensions={0}, use_global_device_ids=true | all-gather | bytes 135168 | tf_op jit(solution)/shard_map/all_gather | solution.py:334
  91.2 0.1 constant_dynamic-slice_fusion
  91.3 0.0 copy-start.1
  91.4 0.0 copy-done.5
  91.4 0.0 copy-done.6
  91.4 0.0 copy-done.8
  91.4 0.0 copy-done.9
  91.4 0.0 copy-done.12
  91.4 0.0 copy-done.13
  91.4 13.7 %column_attention.1 = (bf16[32,32,256]{2,1,0:T(8,128)(2,1)S(1)}, bf16[8,32,128]{2,1,0:T(8,128)(2,1)S(1)}, bf16[256,128]{1,0:T(8,128)(2,1)S(1)}) custom-call(bf16[32,32,256]{2,1,0:T(8,128)(2,1)S(1)} %to_columns.1.in_ref, f32[8,1,128]{2,1,0:T(1,128)S(1)} %bitcast.31, f32[1,256]{1,0:T(1,128)S(1)} %bitcast.34, bf16[256,512]{1,0:T(8,128)(2,1)S(1)} %copy-done.5, ...), custom_call_target="tpu_custom_call" | custom-call | tf_op jit(solution)/shard_map/column_attention/pallas_call | solution.py:389
  105.1 24.0 %spread.1 = (bf16[32,32,256]{2,1,0:T(8,128)(2,1)S(1)}, bf16[32,256,128]{2,1,0:T(8,128)(2,1)S(1)}) custom-call(bf16[32,32,256]{2,1,0:T(8,128)(2,1)S(1)} %get-tuple-element.7.new_ref, bf16[256,128]{1,0:T(8,128)(2,1)S(1)} %get-tuple-element.8.right_ref), custom_call_target="tpu_custom_call" | custom-call | tf_op jit(solution)/shard_map/spread/pallas_call | solution.py:417
  129.1 0.8 copy_bitcast_fusion
  129.9 1.1 copy.35
  131.0 0.1 copy.36.weight_ref
  131.2 0.1 dynamic_slice.7
  131.2 0.2 fusion.scale_ref
  131.4 0.0 copy-done.1
  131.4 2.7 %outer_product.1 = bf16[8,256,128]{2,1,0:T(8,128)(2,1)} custom-call(bf16[8,32,128]{2,1,0:T(8,128)(2,1)S(1)} %get-tuple-element.10.left_ref, bf16[32,256,128]{2,1,0:T(8,128)(2,1)S(1)} %get-tuple-element.11.right_ref, bf16[128,1024]{1,0:T(8,128)(2,1)S(1)} %copy.36.weight_ref, f32[8,256]{1,0:T(8,128)S(1)} %fusion.scale_ref, bf16[8,256,128]{2,1,0:T(8,128)(2,1)S(1)} %copy-done.1), custom_call_target="tpu_custom_call" | custom-call | tf_op jit(solution)/shard_map/outer_product/pallas_call | solution.py:427
  (4 shorter events, 0.1 us)
Async XLA Ops:
  0.6 1.0 copy-start
  1.7 0.7 copy-start.10
  2.4 0.7 copy-start.14
  21.1 1.0 copy-start.2
  22.1 0.9 copy-start.3
  23.1 0.9 copy-start.4
  24.0 0.9 copy-start.7
  24.9 0.7 copy-start.11
  25.6 21.8 %copy-start.15 = (s32[4,256]{1,0:T(4,128)S(1)}, s32[4,256]{1,0:T(4,128)}, u32[]{:S(2)}) copy-start(s32[4,256]{1,0:T(4,128)} %param.19) | copy-start | bytes 12292
  33.8 57.6 %copy-start.5 = (bf16[256,512]{1,0:T(8,128)(2,1)S(1)}, bf16[256,512]{1,0:T(8,128)(2,1)}, u32[]{:S(2)}) copy-start(bf16[256,512]{1,0:T(8,128)(2,1)} %scoring_ref.3) | copy-start | bytes 786436
  33.8 57.6 %copy-start.6 = (bf16[256,512]{1,0:T(8,128)(2,1)S(1)}, bf16[256,512]{1,0:T(8,128)(2,1)}, u32[]{:S(2)}) copy-start(bf16[256,512]{1,0:T(8,128)(2,1)} %values_ref.3) | copy-start | bytes 786436
  33.8 57.6 %copy-start.8 = (bf16[256,256]{1,0:T(8,128)(2,1)S(1)}, bf16[256,256]{1,0:T(8,128)(2,1)}, u32[]{:S(2)}) copy-start(bf16[256,256]{1,0:T(8,128)(2,1)} %output_ref.3) | copy-start | bytes 393220
  33.8 57.6 %copy-start.9 = (bf16[256,64]{0,1:T(8,128)(2,1)S(1)}, bf16[256,64]{0,1:T(8,128)(2,1)}, u32[]{:S(2)}) copy-start(bf16[256,64]{0,1:T(8,128)(2,1)} %param.32) | copy-start | bytes 98308
  33.8 57.6 %copy-start.12 = (f32[256]{0:T(256)S(1)}, f32[256]{0:T(256)}, u32[]{:S(2)}) copy-start(f32[256]{0:T(256)} %param.27) | copy-start | bytes 3076
  33.8 57.6 %copy-start.13 = (f32[256]{0:T(256)S(1)}, f32[256]{0:T(256)}, u32[]{:S(2)}) copy-start(f32[256]{0:T(256)} %param.31) | copy-start | bytes 3076
  91.3 40.1 %copy-start.1 = (bf16[8,256,128]{2,1,0:T(8,128)(2,1)S(1)}, bf16[8,256,128]{2,1,0:T(8,128)(2,1)}, u32[]{:S(2)}) copy-start(bf16[8,256,128]{2,1,0:T(8,128)(2,1)} %pair_ref.3) | copy-start | bytes 1572868

commit v2 on v1

v2 whole, which is shorter than its diff:
```python
import functools
import math

import jax
import jax.numpy as jnp
from jax import lax
from jax.experimental import pallas as pl
from jax.experimental.pallas import tpu as pltpu
from jax.sharding import PartitionSpec as P

HEADS = 8
HEAD = 32
C_OPM = 32
LOG2E = math.log2(math.e)
SCALE = LOG2E / math.sqrt(HEAD)
MASKED = -1000000000.0 * LOG2E
NT = (((1,), (1,)), ((), ()))
MESH = pl.DeviceIdType.MESH
VMEM = pl.BlockSpec(memory_space=pltpu.VMEM)
LIMIT = 48 * 1024 * 1024


def norm(wide, gain):
    average = jnp.mean(wide, axis=-1, keepdims=True)
    centred = wide - average
    spread = jnp.mean(centred * centred, axis=-1, keepdims=True)
    return (centred * lax.rsqrt(spread + 1e-05) * gain).astype(jnp.bfloat16)


def dot(a, b):
    return jnp.dot(a, b, preferred_element_type=jnp.float32)


def dot_nt(a, b):
    return lax.dot_general(a, b, NT, preferred_element_type=jnp.float32)


def greet_all(n, me):
    barrier = pltpu.get_barrier_semaphore()

    def one(k, carry):
        pl.semaphore_signal(
            barrier, inc=1, device_id={"dap": lax.rem(me + k, n)}, device_id_type=MESH
        )
        return carry

    lax.fori_loop(1, n, one, 0)


def met_all(n):
    pl.semaphore_wait(pltpu.get_barrier_semaphore(), n - 1)


class Gather:
    def __init__(self, n, me, out, zs, zr, ps, pr, cs, cr):
        self.n, self.me, self.out = n, me, out
        self.sems = {"z": (zs, zr), "p": (ps, pr), "c": (cs, cr)}
        self.layers = n // 8
        self.z = me // 8
        self.p = lax.rem(me // 2, 4)
        self.c = lax.rem(me, 2)

    def place(self, z, p, c):
        return z * 8 + p * 2 + c

    def plane(self, p, k):
        if k == 0:
            return p
        if k == 1:
            return p + 1 - 2 * lax.rem(p, 2)
        if k == 2:
            return lax.rem(p + 2, 4)
        return 3 - p

    def copy(self, kind, slot, block, target):
        send, recv = self.sems[kind]
        return pltpu.make_async_remote_copy(
            src_ref=self.out.at[block],
            dst_ref=self.out.at[block],
            send_sem=send.at[slot],
            recv_sem=recv.at[slot],
            device_id={"dap": target},
            device_id_type=MESH,
        )

    def layer(self, d):
        return lax.rem(self.z + self.layers - d, self.layers)

    def z_copy(self, d):
        return self.copy("z", d, self.me, self.place(lax.rem(self.z + d, self.layers), self.p, self.c))

    def p_copy(self, d, k):
        block = self.place(self.layer(d), self.p, self.c)
        return self.copy("p", d * 4 + k, block, self.place(self.z, self.plane(self.p, k), self.c))

    def c_copy(self, d, k):
        block = self.place(self.layer(d), self.plane(self.p, k), self.c)
        return self.copy("c", d * 4 + k, block, self.place(self.z, self.p, 1 - self.c))

    def z_arrived(self, d):
        block = self.place(self.layer(d), self.p, self.c)
        self.copy("z", d, block, self.place(lax.rem(self.z + d, self.layers), self.p, self.c)).wait_recv()

    def p_arrived(self, d, k):
        block = self.place(self.layer(d), self.plane(self.p, k), self.c)
        self.copy("p", d * 4 + k, block, self.place(self.z, self.plane(self.p, k), self.c)).wait_recv()

    def c_arrived(self, d, k):
        block = self.place(self.layer(d), self.plane(self.p, k), 1 - self.c)
        self.copy("c", d * 4 + k, block, self.place(self.z, self.p, 1 - self.c)).wait_recv()

    def start(self):
        for d in range(1, self.layers):
            self.z_copy(d).start()
        for k in (1, 2, 3):
            self.p_copy(0, k).start()
        self.c_copy(0, 0).start()

    def relay_layers(self):
        for d in range(1, self.layers):
            self.z_arrived(d)
            for k in (1, 2, 3):
                self.p_copy(d, k).start()
            self.c_copy(d, 0).start()

    def relay_plane(self):
        for d in range(self.layers):
            for k in (1, 2, 3):
                self.p_arrived(d, k)
                self.c_copy(d, k).start()

    def finish(self):
        for d in range(self.layers):
            for k in range(4):
                self.c_arrived(d, k)
        for d in range(self.layers):
            if d > 0:
                self.z_copy(d).wait_send()
            for k in range(4):
                if k > 0:
                    self.p_copy(d, k).wait_send()
                self.c_copy(d, k).wait_send()


def gather_sems(n):
    layers = n // 8
    sizes = (layers, layers, layers * 4, layers * 4, layers * 4, layers * 4)
    return [pltpu.SemaphoreType.DMA((size,)) for size in sizes]


class Exchange:
    def __init__(self, n, me, src, dst, piece, send, recv):
        self.n, self.me, self.src, self.dst = n, me, src, dst
        self.rows, self.first = pl.ds(piece * 16, 16), piece * n
        self.send, self.recv = send, recv

    def copy(self, k, block_out, block_in):
        return pltpu.make_async_remote_copy(
            src_ref=self.src.at[block_out, self.rows],
            dst_ref=self.dst.at[block_in, self.rows],
            send_sem=self.send.at[self.first + k],
            recv_sem=self.recv.at[self.first + k],
            device_id={"dap": block_out},
            device_id_type=MESH,
        )

    def start(self):
        def one(k, carry):
            self.copy(k, lax.rem(self.me + k, self.n), self.me).start()
            return carry

        lax.fori_loop(1, self.n, one, 0)
        self.dst[self.me, self.rows] = self.src[self.me, self.rows]

    def finish(self):
        def one(k, carry):
            target = lax.rem(self.me + k, self.n)
            self.copy(k, target, lax.rem(self.me + self.n - k, self.n)).wait_recv()
            self.copy(k, target, self.me).wait_send()
            return carry

        lax.fori_loop(1, self.n, one, 0)


def attend(joint, gated, keeps, width, bias):
    queries, keys_all = joint[:, :width], joint[:, width:]
    values_all, gates = gated[:, :width], gated[:, width:]
    groups = len(keeps)
    length = joint.shape[0] // groups
    lanes = lax.broadcasted_iota(jnp.int32, (1, width), 1) // HEAD
    totals = [None] * groups
    for h in range(HEADS):
        mine = (lanes == h).astype(jnp.float32).astype(jnp.bfloat16)
        asked, given = queries * mine, values_all * mine
        for g in range(groups):
            part = slice(g * length, (g + 1) * length)
            scores = dot_nt(asked[part], keys_all[part]) * SCALE
            if bias is not None:
                scores = scores + bias(h)
            scores = jnp.where(keeps[g], scores, MASKED)
            powers = jnp.exp2(scores - jnp.max(scores, axis=-1, keepdims=True))
            weights = powers * (1.0 / jnp.sum(powers, axis=-1, keepdims=True))
            mixed = dot(weights.astype(jnp.bfloat16), given[part])
            totals[g] = mixed if totals[g] is None else totals[g] + mixed
    total = jnp.concatenate(totals, axis=0) if groups > 1 else totals[0]
    return (total * jax.nn.sigmoid(gates.astype(jnp.float32))).astype(jnp.bfloat16)


N_IN = 17


def kernel(n, *refs):
    inputs, (back, new_pair), scratch = refs[:N_IN], refs[N_IN : N_IN + 2], refs[N_IN + 2 :]
    held, scratch = scratch[:N_IN], scratch[N_IN:]
    (
        turned, every_bias, wide_bias, joints, gates, stage, sent, columns, wide, turned_right,
        new_sent, left, every_right, wide_right, products, wide_output, turned_output, in_sems,
        ex_send, ex_recv, back_send, back_recv, *sems,
    ) = scratch
    (
        alignment, pair_rep, align_mask, residue_mask, row_gain, pair_gain, row_bias, row_scoring,
        row_values, row_output, column_gain, column_scoring, column_values, column_output,
        outer_gain, outer_inputs, outer_output,
    ) = held
    narrow, full = jnp.bfloat16, jnp.float32
    me = lax.axis_index("dap")
    seqs, total_res, width = alignment.shape
    rows = pair_rep.shape[0]
    total_seqs = seqs * n
    half = rows // 2

    order = (1, 5, 6, 2, 0, 4, 7, 8, 3, 9, 10, 11, 12, 13, 14, 15, 16)
    loads = [pltpu.make_async_copy(inputs[k], held[k], in_sems.at[k]) for k in range(N_IN)]
    for k in order:
        loads[k].start()
    greet_all(n, me)

    for k in (1, 5, 6, 2):
        loads[k].wait()
    for i in range(rows):
        normed = norm(pair_rep[i].astype(full), pair_gain[...])
        turned[:HEADS, i, :] = dot_nt(row_bias[...], normed)
    turned[HEADS] = jnp.zeros(turned.shape[1:], full)
    turned[HEADS + 1] = jnp.zeros(turned.shape[1:], full)
    turned[HEADS, :seqs, :] = align_mask[...].astype(full)
    every_bias[me] = turned[...].reshape(every_bias.shape[1:]).astype(narrow)
    met_all(n)
    gather = Gather(n, me, every_bias, *sems[:6])
    gather.start()

    def project(s, carry):
        normed = norm(alignment[s].astype(full), row_gain[...])
        joints[s] = dot(normed, row_scoring[...]).astype(narrow)
        gates[s] = dot(normed, row_values[...]).astype(narrow)
        return carry

    for k in (0, 4, 7, 8):
        loads[k].wait()
    lax.fori_loop(0, seqs // 2, project, 0)
    gather.relay_layers()
    lax.fori_loop(seqs // 2, seqs, project, 0)
    gather.relay_plane()
    for k in (3, 9, 10, 11, 12, 13, 14, 15, 16):
        loads[k].wait()
    wide_output[...] = outer_output[...].astype(full).reshape(wide_output.shape)
    for g in range(C_OPM // 4):
        piece = jnp.concatenate([wide_output[:, g * 4 + t, :] for t in range(4)], axis=0)
        turned_output[:, g * 128 : (g + 1) * 128] = piece.T.astype(narrow)
    gather.finish()

    wide_bias[...] = every_bias[:, : HEADS * rows, :].astype(full) * LOG2E
    every_mask = every_bias[:, HEADS * rows :, :].astype(full)[:, :rows, :].reshape(n * rows, total_res)
    place = lax.broadcasted_iota(jnp.int32, (total_seqs, n * rows), 0)
    spot = lax.broadcasted_iota(jnp.int32, (total_seqs, n * rows), 1)
    pick = (spot == place // seqs * rows + place % seqs).astype(full).astype(narrow)
    mask = dot(pick, every_mask.astype(narrow)).astype(narrow)
    near = lax.broadcasted_iota(jnp.int32, (rows, total_res), 1) - me * rows
    own = (near == lax.broadcasted_iota(jnp.int32, (rows, total_res), 0)).astype(full)
    keep_columns = dot_nt(own.astype(narrow), mask)
    residue_float = residue_mask[...].astype(full)
    row_factor = jnp.sum(own * residue_float, axis=-1, keepdims=True)
    pair_count = dot(keep_columns.astype(narrow), mask)
    scale = row_factor * residue_float / (0.001 + pair_count)

    def bias(h):
        return wide_bias[:, h * rows : (h + 1) * rows, :].reshape(total_res, total_res)

    to_columns = []
    for piece in range(2):
        for t in range(2):
            s = piece * 2 + t
            keep = align_mask[s : s + 1, :].astype(full) * residue_float
            mixed = attend(joints[s], gates[s], [keep > 0], width, bias)
            updated = alignment[s].astype(full) + dot(mixed, row_output[...])
            stage[:, t] = updated.reshape(n, rows, width)
        sent[:, piece * 16 : (piece + 1) * 16, :] = stage[...].reshape(n, 16, width).astype(narrow)
        to_columns.append(Exchange(n, me, sent, columns, piece, ex_send, ex_recv))
        to_columns[piece].start()
    for piece in range(2):
        to_columns[piece].finish()

    wide[...] = columns[...].astype(full).reshape(wide.shape)
    backwards = []
    for piece in range(2):
        mine = range(piece * half, (piece + 1) * half)
        stream = jnp.concatenate([wide[:, i, :] for i in mine], axis=0)
        normed = norm(stream, column_gain[...])
        joint = dot(normed, column_scoring[...]).astype(narrow)
        gated = dot(normed, column_values[...]).astype(narrow)
        keeps = [keep_columns[i : i + 1, :] > 0 for i in mine]
        mixed = attend(joint, gated, keeps, width, None)
        second = (stream + dot(mixed, column_output[...])).astype(narrow).astype(full)
        outer_normed = norm(second, outer_gain[...])
        for t, i in enumerate(mine):
            part = slice(t * total_seqs, (t + 1) * total_seqs)
            sides = dot_nt(outer_inputs[...], outer_normed[part]) * keep_columns[i : i + 1, :]
            left[i] = sides[:C_OPM].astype(narrow)
            turned_right[:, i, :] = sides[C_OPM:]
            wide[:, i, :] = second[part]
        block = wide[:, piece * half : (piece + 1) * half, :].reshape(n, 16, width)
        new_sent[:, piece * 16 : (piece + 1) * 16, :] = block.astype(narrow)
        backwards.append(Exchange(n, me, new_sent, back, piece, back_send, back_recv))
        if piece == 0:
            backwards[0].start()
    every_right[me] = turned_right[...].reshape(every_right.shape[1:]).astype(narrow)
    gather = Gather(n, me, every_right, *sems[6:])
    gather.start()
    gather.relay_layers()
    gather.relay_plane()
    backwards[1].start()
    gather.finish()

    sides = left[...].reshape(rows * C_OPM, total_seqs)
    wide_right[...] = every_right[...].astype(full)
    for e in range(C_OPM):
        piece = wide_right[:, e * rows : (e + 1) * rows, :].reshape(total_res, total_seqs)
        block = dot_nt(sides, piece.astype(narrow)).astype(narrow)
        products[:, e * C_OPM : (e + 1) * C_OPM, :] = block.reshape(rows, C_OPM, total_res)
    for i in range(rows):
        flat = dot(turned_output[...], products[i]) * scale[i : i + 1, :]
        new_pair[i] = (pair_rep[i].astype(full) + flat.T).astype(narrow)
    for piece in range(2):
        backwards[piece].finish()


def body(n, alignment, pair_rep, align_mask, residue_mask, *rest):
    (
        row_gain, pair_gain, row_bias, row_scoring, row_values, row_output, column_gain,
        column_scoring, column_values, column_output, outer_gain, outer_inputs, outer_output,
    ) = rest
    seqs, total_res, width = alignment.shape
    rows, _, channels = pair_rep.shape
    total_seqs = seqs * n
    narrow, full = jnp.bfloat16, jnp.float32
    arguments = (
        alignment, pair_rep, align_mask, residue_mask[None], row_gain[None], pair_gain[None],
        row_bias.T, row_scoring, row_values, row_output, column_gain[None], column_scoring,
        column_values, column_output, outer_gain[None], outer_inputs.T, outer_output,
    )
    dma = pltpu.SemaphoreType.DMA
    blocks = (n, seqs * rows, width)
    right_shape = (C_OPM * rows, total_seqs)
    flat = C_OPM * C_OPM
    back, new_pair = pl.pallas_call(
        functools.partial(kernel, n),
        out_shape=(
            jax.ShapeDtypeStruct(blocks, narrow),
            jax.ShapeDtypeStruct(pair_rep.shape, narrow),
        ),
        in_specs=[pl.BlockSpec(memory_space=pl.ANY)] * N_IN,
        out_specs=(VMEM, VMEM),
        scratch_shapes=[pltpu.VMEM(array.shape, array.dtype) for array in arguments]
        + [
            pltpu.VMEM((HEADS + 2, rows, total_res), full),
            pltpu.VMEM((n, (HEADS + 2) * rows, total_res), narrow),
            pltpu.VMEM((n, HEADS * rows, total_res), full),
            pltpu.VMEM((seqs, total_res, 2 * width), narrow),
            pltpu.VMEM((seqs, total_res, 2 * width), narrow),
            pltpu.VMEM((n, 2, rows, width), full),
            pltpu.VMEM(blocks, narrow),
            pltpu.VMEM(blocks, narrow),
            pltpu.VMEM((total_seqs, rows, width), full),
            pltpu.VMEM((C_OPM, rows, total_seqs), full),
            pltpu.VMEM(blocks, narrow),
            pltpu.VMEM((rows, C_OPM, total_seqs), narrow),
            pltpu.VMEM((n,) + right_shape, narrow),
            pltpu.VMEM((n,) + right_shape, full),
            pltpu.VMEM((rows, flat, total_res), narrow),
            pltpu.VMEM((C_OPM, C_OPM, channels), full),
            pltpu.VMEM((channels, flat), narrow),
            dma((N_IN,)),
        ]
        + [dma((2 * n,))] * 4
        + gather_sems(n)
        + gather_sems(n),
        compiler_params=pltpu.CompilerParams(
            vmem_limit_bytes=LIMIT, collective_id=0, has_side_effects=True
        ),
        name="evoformer",
    )(*arguments)
    back = back.reshape(n, 2, seqs, rows // 2, width).transpose(2, 0, 1, 3, 4)
    return back.reshape(alignment.shape), new_pair


def solution(mesh):
    split = P(("dp", "dap"), None, None)
    in_specs = (split, split, P(("dp", "dap"), None), P("dp")) + (P(),) * 13
    return jax.shard_map(
        functools.partial(body, mesh.shape["dap"]),
        mesh=mesh,
        in_specs=in_specs,
        out_specs=(split, split),
        check_vma=False,
    )
```

time: 135 us -> 86 us (0.64)
  blocking collectives: 43.7 us -> 0 us
  Pallas kernels: 78.7 us -> 72.6 us
  local copies, waits for them, and re-layouts: 9.31 us -> 12.1 us
  other arithmetic: 1.4 us -> 0 us
    all_gather x1 -> x0, blocking collectives: 43.7 us -> none  [body(): lax.all_gather(align_mask, 'dap', axis=0, tiled=True).astype(wide)]
    pallas_call x6 -> x1, Pallas kernels: 78.7 us -> 72.6 us  [body(): pl.pallas_call(functools.partial(kernel, n), out_shape=(jax.ShapeDtypeStr...]
    unnamed x34 -> x35, local copies, waits for them, and re-layouts: 7.09 us -> 10.9 us
where the time goes in v2:
time: 86 us; the launch traced here: 85.5 us
  Pallas kernels  72.6 us (84%)
  local copies, waits for them, and re-layouts  12.1 us (14%)
    pallas_call x1, Pallas kernels, body(): pl.pallas_call(functools.partial(kernel, n), out_shape=(jax.ShapeDtypeStr...  72.6 us
    unnamed x35, local copies, waits for them, and re-layouts  10.9 us

profile of v2, /device:TPU:0, one launch (start us, length us, event | category | flops | bytes accessed | tf_op | source)
XLA Modules:
  0.0 85.5 jit_solution(1582858686639595575)
XLA Ops:
  0.6 0.0 copy-start.15
  0.6 0.0 copy-start.16
  0.7 0.0 copy-start.13
  0.7 0.0 copy-start.14
  0.7 0.0 copy-start.10
  0.7 0.0 copy-start.11
  0.7 0.0 copy-start.12
  0.7 0.6 copy-done.15
  1.3 0.0 copy-done.16
  1.3 0.0 copy-done.13
  1.3 0.0 copy-done.14
  1.4 0.0 copy-done.10
  1.4 0.0 copy-done.11
  1.4 0.0 copy-done.12
  1.4 0.0 copy-start
  1.4 1.0 %copy-done = bf16[4,256,256]{2,1,0:T(8,128)(2,1)S(1)} copy-done((bf16[4,256,256]{2,1,0:T(8,128)(2,1)S(1)}, bf16[4,256,256]{2,1,0:T(8,128)(2,1)}, u32[]{:S(2)}) %copy-start) | copy-done | bytes 524312
  2.5 0.0 copy-start.1
  2.5 1.0 %copy-done.1 = bf16[8,256,128]{2,1,0:T(8,128)(2,1)S(1)} copy-done((bf16[8,256,128]{2,1,0:T(8,128)(2,1)S(1)}, bf16[8,256,128]{2,1,0:T(8,128)(2,1)}, u32[]{:S(2)}) %copy-start.1) | copy-done | bytes 524312
  3.5 0.0 copy-start.2
  3.5 0.9 %copy-done.2 = bf16[256,512]{1,0:T(8,128)(2,1)S(1)} copy-done((bf16[256,512]{1,0:T(8,128)(2,1)S(1)}, bf16[256,512]{1,0:T(8,128)(2,1)}, u32[]{:S(2)}) %copy-start.2) | copy-done | bytes 262168
  4.4 0.0 copy-start.3
  4.4 0.9 %copy-done.3 = bf16[256,512]{1,0:T(8,128)(2,1)S(1)} copy-done((bf16[256,512]{1,0:T(8,128)(2,1)S(1)}, bf16[256,512]{1,0:T(8,128)(2,1)}, u32[]{:S(2)}) %copy-start.3) | copy-done | bytes 262168
  5.4 0.0 copy-start.4
  5.4 0.9 %copy-done.4 = bf16[256,512]{1,0:T(8,128)(2,1)S(1)} copy-done((bf16[256,512]{1,0:T(8,128)(2,1)S(1)}, bf16[256,512]{1,0:T(8,128)(2,1)}, u32[]{:S(2)}) %copy-start.4) | copy-done | bytes 262168
  6.3 0.0 copy-start.5
  6.3 0.9 %copy-done.5 = bf16[256,512]{1,0:T(8,128)(2,1)S(1)} copy-done((bf16[256,512]{1,0:T(8,128)(2,1)S(1)}, bf16[256,512]{1,0:T(8,128)(2,1)}, u32[]{:S(2)}) %copy-start.5) | copy-done | bytes 262168
  7.3 0.0 copy-start.6
  7.3 0.9 %copy-done.6 = bf16[1024,128]{1,0:T(8,128)(2,1)S(1)} copy-done((bf16[1024,128]{1,0:T(8,128)(2,1)S(1)}, bf16[1024,128]{1,0:T(8,128)(2,1)}, u32[]{:S(2)}) %copy-start.6) | copy-done | bytes 262168
  8.2 0.0 copy-start.7
  8.3 0.9 %copy-done.7 = bf16[256,256]{1,0:T(8,128)(2,1)S(1)} copy-done((bf16[256,256]{1,0:T(8,128)(2,1)S(1)}, bf16[256,256]{1,0:T(8,128)(2,1)}, u32[]{:S(2)}) %copy-start.7) | copy-done | bytes 131096
  9.2 0.0 copy-start.8
  9.2 0.9 %copy-done.8 = bf16[256,256]{1,0:T(8,128)(2,1)S(1)} copy-done((bf16[256,256]{1,0:T(8,128)(2,1)S(1)}, bf16[256,256]{1,0:T(8,128)(2,1)}, u32[]{:S(2)}) %copy-start.8) | copy-done | bytes 131096
  10.1 0.0 copy-start.9
  10.1 0.8 copy-done.9
  10.8 72.6 %evoformer.1 = (bf16[32,32,256]{2,1,0:T(8,128)(2,1)S(1)}, bf16[8,256,128]{2,1,0:T(8,128)(2,1)S(1)}) custom-call(bf16[4,256,256]{2,1,0:T(8,128)(2,1)S(1)} %copy-done, bf16[8,256,128]{2,1,0:T(8,128)(2,1)S(1)} %copy-done.1, s32[4,256]{1,0:T(4,128)S(1)} %copy-done.10, s32[1,256]{1,0:T(1,128)S(1)} %bitcast.10, f32[1,256]{1,0:T(1,128)S(1)} %bitcast.11, ...), custom_call_target="tpu_custom_call" | custom-call | tf_op jit(solution)/shard_map/evoformer/pallas_call | solution.py:364
  83.5 0.1 reshape.10
  83.6 0.2 copy.19
  83.8 0.9 %reshape.11 = bf16[4,256,256]{2,1,0:T(8,128)(2,1)} reshape(bf16[4,32,2,4,256]{4,3,2,1,0:T(4,128)(2,1)S(1)} %copy.19) | data formatting | bytes 1048576 | tf_op jit(solution)/shard_map/reshape | solution.py:402
  84.7 0.8 copy.21
Async XLA Ops:
  0.6 0.7 copy-start.15
  0.6 0.7 copy-start.16
  0.7 0.7 copy-start.13
  0.7 0.7 copy-start.14
  0.7 0.7 copy-start.10
  0.7 0.7 copy-start.11
  0.7 0.7 copy-start.12
  1.4 1.0 %copy-start = (bf16[4,256,256]{2,1,0:T(8,128)(2,1)S(1)}, bf16[4,256,256]{2,1,0:T(8,128)(2,1)}, u32[]{:S(2)}) copy-start(bf16[4,256,256]{2,1,0:T(8,128)(2,1)} %refs_0_.1) | copy-start | bytes 1572868
  2.5 1.0 %copy-start.1 = (bf16[8,256,128]{2,1,0:T(8,128)(2,1)S(1)}, bf16[8,256,128]{2,1,0:T(8,128)(2,1)}, u32[]{:S(2)}) copy-start(bf16[8,256,128]{2,1,0:T(8,128)(2,1)} %refs_1_.1) | copy-start | bytes 1572868
  3.5 0.9 %copy-start.2 = (bf16[256,512]{1,0:T(8,128)(2,1)S(1)}, bf16[256,512]{1,0:T(8,128)(2,1)}, u32[]{:S(2)}) copy-start(bf16[256,512]{1,0:T(8,128)(2,1)} %refs_7_.1) | copy-start | bytes 786436
  4.4 0.9 %copy-start.3 = (bf16[256,512]{1,0:T(8,128)(2,1)S(1)}, bf16[256,512]{1,0:T(8,128)(2,1)}, u32[]{:S(2)}) copy-start(bf16[256,512]{1,0:T(8,128)(2,1)} %refs_8_.1) | copy-start | bytes 786436
  5.4 0.9 %copy-start.4 = (bf16[256,512]{1,0:T(8,128)(2,1)S(1)}, bf16[256,512]{1,0:T(8,128)(2,1)}, u32[]{:S(2)}) copy-start(bf16[256,512]{1,0:T(8,128)(2,1)} %refs_11_.1) | copy-start | bytes 786436
  6.3 0.9 %copy-start.5 = (bf16[256,512]{1,0:T(8,128)(2,1)S(1)}, bf16[256,512]{1,0:T(8,128)(2,1)}, u32[]{:S(2)}) copy-start(bf16[256,512]{1,0:T(8,128)(2,1)} %refs_12_.1) | copy-start | bytes 786436
  7.3 0.9 %copy-start.6 = (bf16[1024,128]{1,0:T(8,128)(2,1)S(1)}, bf16[1024,128]{1,0:T(8,128)(2,1)}, u32[]{:S(2)}) copy-start(bf16[1024,128]{1,0:T(8,128)(2,1)} %refs_16_.1) | copy-start | bytes 786436
  8.2 0.9 %copy-start.7 = (bf16[256,256]{1,0:T(8,128)(2,1)S(1)}, bf16[256,256]{1,0:T(8,128)(2,1)}, u32[]{:S(2)}) copy-start(bf16[256,256]{1,0:T(8,128)(2,1)} %refs_9_.1) | copy-start | bytes 393220
  9.2 0.9 %copy-start.8 = (bf16[256,256]{1,0:T(8,128)(2,1)S(1)}, bf16[256,256]{1,0:T(8,128)(2,1)}, u32[]{:S(2)}) copy-start(bf16[256,256]{1,0:T(8,128)(2,1)} %refs_13_.1) | copy-start | bytes 393220
  10.1 0.8 copy-start.9
